TPU v7x, 32 devices: a whole 2x2x4 slice. The times are simulated.
32 devices in a mesh: seq: 8 (over z, y), head: 4 (over x, core).
Axes of the slice: x: 2, y: 2, z: 4, core: 2. Of those that a mesh axis runs over, the one named last changes fastest.
Arguments:
- queries: bfloat16 [4096, 2048], P('seq', 'head'), may hold values from -6 to 6
- key_pairs: bfloat16 [4096, 2, 2048], P('seq', None, 'head'), may hold values from -6 to 6
- value_pairs: bfloat16 [4096, 2, 2048], P('seq', None, 'head'), may hold values from -0.375 to 0.375
- init_state: float32 [16, 128, 128], P('head'), may hold values from -6 to 6
- out_weight: bfloat16 [2048, 2048], replicated, may hold values from -0.125 to 0.125
Outputs:
- projected: bfloat16 [4096, 2048], P('seq', 'head')
All inputs are finite; a program needn't handle non-finite values.
Results may differ from a plain program's by a relative error of at most 0.0085.
Values may be sent and summed in bfloat16 or wider, within the bound.
A program may use at most 128 MiB of HBM per device.

v0:
```python
import jax
import jax.numpy as jnp
from jax import lax
from jax.sharding import PartitionSpec as P

HEAD_DIM = 128
BLOCK = 32


epsilon = 1e-06


def carried_in(part, axis, combine, identity):
    place = lax.axis_index(axis)
    gathered = jax.tree.map(lambda a: lax.all_gather(a, axis), part)
    state = jax.tree.map(lambda a, e: jnp.zeros_like(a) + jnp.asarray(e, a.dtype), part, identity)

    def one(hop, state):
        return combine(
            state, jax.tree.map(lambda a: lax.dynamic_index_in_dim(a, hop, 0, False), gathered)
        )

    return lax.fori_loop(0, place, one, state)


def product(left, right, pattern):
    return jnp.einsum(pattern, left, right, precision=lax.Precision.HIGHEST)


def unit_rows(entries):
    return entries * lax.rsqrt(jnp.sum(entries * entries, axis=-1, keepdims=True) + epsilon)


def block_parts(query_block, key_block, value_block):
    query_block = unit_rows(query_block.astype(jnp.float32))
    key_block = unit_rows(key_block.astype(jnp.float32))
    value_block = value_block.astype(jnp.float32)
    state_width = key_block.shape[-1]
    micro_len = key_block.shape[-2]
    gram = product(key_block, key_block, "...id,...jd->...ij")
    strict = jnp.tril(jnp.ones((micro_len, micro_len), jnp.float32), -1)
    system = jnp.eye(micro_len, dtype=jnp.float32) + 2.0 * gram * strict
    stacked = 2.0 * jnp.concatenate([key_block, value_block], axis=-1)
    solved = jax.scipy.linalg.solve_triangular(system, stacked, lower=True, unit_diagonal=True)
    writes = solved[..., :state_width]
    updates = solved[..., state_width:]
    scores = product(query_block, key_block, "...id,...jd->...ij")
    row_index = lax.broadcasted_iota(jnp.int32, (query_block.shape[-2], micro_len), 0)
    col_index = lax.broadcasted_iota(jnp.int32, (query_block.shape[-2], micro_len), 1)
    scores = jnp.where(col_index <= 2 * row_index + 1, scores, jnp.zeros_like(scores))
    adjusted = query_block - product(scores, writes, "...ij,...jd->...id")
    inside = product(scores, updates, "...ij,...jd->...id")
    moving = jnp.eye(state_width, dtype=jnp.float32) - product(
        key_block, writes, "...cd,...ce->...de"
    )
    carried = product(key_block, updates, "...cd,...ce->...de")
    return (adjusted, inside, moving, carried)


def compose(earlier, later):
    return (
        product(later[0], earlier[0], "...ij,...jk->...ik"),
        product(later[0], earlier[1], "...ij,...jk->...ik") + later[1],
    )


def advance_map(running_map, pieces):
    return (compose(running_map, pieces), running_map)


def local(queries, key_pairs, value_pairs, init_state, out_weight):
    tokens = queries.shape[0]
    head_count = queries.shape[1] // HEAD_DIM
    blocks = tokens // BLOCK
    state_width = HEAD_DIM
    query_blocks = jnp.transpose(queries.reshape(blocks, BLOCK, head_count, HEAD_DIM), (2, 0, 1, 3))
    key_blocks = jnp.transpose(
        key_pairs.reshape(blocks, 2 * BLOCK, head_count, HEAD_DIM), (2, 0, 1, 3)
    )
    value_blocks = jnp.transpose(
        value_pairs.reshape(blocks, 2 * BLOCK, head_count, HEAD_DIM), (2, 0, 1, 3)
    )
    adjusted, inside, moving, carried = block_parts(query_blocks, key_blocks, value_blocks)
    per_group = 8
    group_count = blocks // per_group

    def grouped(array):
        shaped = array.reshape((head_count, group_count, per_group) + array.shape[2:])
        return jnp.moveaxis(shaped, 2, 0)

    identity = jnp.eye(state_width, dtype=jnp.float32)
    group_identity = jnp.broadcast_to(identity, (head_count, group_count, state_width, state_width))
    group_zeros = jnp.zeros((head_count, group_count, state_width, state_width), jnp.float32)
    group_map, start_map = lax.scan(
        advance_map, (group_identity, group_zeros), (grouped(moving), grouped(carried))
    )
    start_move = jnp.moveaxis(start_map[0], 0, 2)
    start_carry = jnp.moveaxis(start_map[1], 0, 2)
    head_identity = jnp.broadcast_to(identity, (head_count, state_width, state_width))
    head_zeros = jnp.zeros((head_count, state_width, state_width), jnp.float32)
    shard_map_pair, prior_map = lax.scan(
        advance_map,
        (head_identity, head_zeros),
        (jnp.moveaxis(group_map[0], 1, 0), jnp.moveaxis(group_map[1], 1, 0)),
    )
    prior_move = jnp.moveaxis(prior_map[0], 0, 1)
    prior_carry = jnp.moveaxis(prior_map[1], 0, 1)
    query_grouped = adjusted.reshape(head_count, group_count, per_group, BLOCK, state_width)
    inside_grouped = inside.reshape(head_count, group_count, per_group, BLOCK, state_width)
    before_move, before_carry = carried_in(
        (shard_map_pair[0], shard_map_pair[1]), "seq", compose, (head_identity, head_zeros)
    )
    entering = product(before_move, init_state, "hij,hjk->hik") + before_carry
    group_state = product(prior_move, entering, "hgij,hjk->hgik") + prior_carry
    block_state = product(start_move, group_state, "hgpij,hgjk->hgpik") + start_carry
    attended_grouped = product(query_grouped, block_state, "hgpcd,hgpde->hgpce") + inside_grouped
    attended_heads = attended_grouped.reshape(head_count, blocks, BLOCK, state_width)
    attended = (
        jnp.transpose(attended_heads, (1, 2, 0, 3))
        .reshape(tokens, head_count * state_width)
        .astype(jnp.bfloat16)
    )
    model_cols = out_weight.shape[1] // lax.axis_size("head")
    own_cols = lax.dynamic_slice_in_dim(
        out_weight, lax.axis_index("head") * model_cols, model_cols, 1
    )
    return jnp.dot(
        lax.all_gather(attended, "head", axis=1, tiled=True),
        own_cols,
        preferred_element_type=jnp.float32,
    ).astype(jnp.bfloat16)


def solution(mesh):
    in_specs = (
        P("seq", "head"),
        P("seq", None, "head"),
        P("seq", None, "head"),
        P("head", None, None),
        P(),
    )
    out_specs = P("seq", "head")
    return jax.shard_map(local, mesh=mesh, in_specs=in_specs, out_specs=out_specs, check_vma=False)
```

profile of v0, /device:TPU:29, one launch (start us, length us, event | category | flops | bytes accessed | tf_op | source)
XLA Modules:
  0.0 590.7 jit_solution(10328810226041184212)
XLA Ops:
  14.9 3.2 copy.61
  18.1 4.7 add_bitcast_fusion
  22.8 316.1 %custom-call.4 = f32[4,16,1,64,64]{3,4,2,1,0:T(8,128)} custom-call(f32[4,16,1,64,64]{4,3,2,1,0:T(8,128)} %add_bitcast_fusion), custom_call_target="InvertDiagBlocksLowerTriangular" | custom-call | tf_op jit(solution)/shard_map/jit(_solve_triangular)/vmap(vmap())/triangular_solve | solution.py:44
  339.0 6.1 %fusion.29 = f32[4,16,64,256]{3,2,1,0:T(8,128)S(1)} fusion(f32[4,16,64,128]{3,2,1,0:T(8,128)} %bitcast.143, f32[4,16,64,128]{3,2,1,0:T(8,128)S(1)} %bitcast_multiply_fusion, f32[4,16,1,64,64]{3,4,2,1,0:T(8,128)} %custom-call.4), kind=kOutput, calls=%fused_computation.37 | convolution fusion | flops 807403520 | bytes 9437184 | tf_op jit(solution)/shard_map/jit(_solve_triangular)/vmap(vmap())/triangular_solve | solution.py:44
  345.1 6.7 %fusion.45 = f32[4,16,128,128]{3,2,1,0:T(8,128)S(1)} fusion(f32[4,16,64,128]{3,2,1,0:T(8,128)S(1)} %bitcast_multiply_fusion, f32[4,16,64,256]{3,2,1,0:T(8,128)S(1)} %fusion.29), kind=kOutput, calls=%fused_computation.59 | convolution fusion | flops 805306368 | bytes 8388608 | tf_op jit(solution)/shard_map/...cd,...ce->...de/dot_general | solution.py:27
  351.9 7.0 %convolution_subtract_fusion = f32[4,16,128,128]{3,2,1,0:T(8,128)S(1)} fusion(f32[4,16,64,128]{3,2,1,0:T(8,128)S(1)} %bitcast_multiply_fusion, f32[128,128]{1,0:T(8,128)S(1)} %fusion.69, f32[4,16,64,256]{3,2,1,0:T(8,128)S(1)} %fusion.29), kind=kOutput, calls=%fused_computation.47 | convolution fusion | flops 806354944 | bytes 8454144 | tf_op jit(solution)/shard_map/...cd,...ce->...de/dot_general | solution.py:27
  363.4 52.1 %while.47 = (s32[]{:T(128)}, f32[4,2,128,128]{3,2,1,0:T(8,128)S(1)}, f32[4,2,128,128]{3,2,1,0:T(8,128)}, f32[8,4,2,128,128]{4,3,2,1,0:T(8,128)}, f32[8,4,2,128,1...) while((s32[]{:T(128)}, ...), condition=%wide.region_3.4_spmd.clone, body=%wide.region_2.3_spmd.clone.sunk | while | flops 403046400 | bytes 7865975 | solution.py:94
  367.3 2.6 convolution_add_fusion.9
  373.8 2.6 convolution_add_fusion.9
  380.3 2.6 convolution_add_fusion.9
  386.8 2.6 convolution_add_fusion.9
  393.3 2.6 convolution_add_fusion.9
  399.8 2.6 convolution_add_fusion.9
  406.3 2.6 convolution_add_fusion.9
  417.4 6.7 %while.48 = (s32[]{:T(128)}, f32[4,128,128]{2,1,0:T(8,128)S(1)}, f32[4,128,128]{2,1,0:T(8,128)}, f32[2,4,128,128]{3,2,1,0:T(8,128)}, f32[2,4,128,128]{3,2,1,0:T(...) while((s32[]{:T(128)}, f32[4,128,128]{2,1,0:T(8,128)S(1)}, ...), condition=%wide.region_5.6_spmd.clone, body=%wide.region_4.5_spmd.clone.sunk | while | flops 201523200 | bytes 6030995 | solution.py:101
  427.9 3.4 convolution_select_fusion
  431.3 3.0 fusion.43
  436.5 36.2 %all-gather.8.cloned.1.call-done = f32[32,128,128]{2,1,0:T(8,128)} async-done(((f32[4,128,128]{2,1,0:T(8,128)}), f32[32,128,128]{2,1,0:T(8,128)}) %all-gather.8.cloned.1.call-update) | async-done | bytes 2097168 | tf_op jit(solution)/shard_map/all_gather | solution.py:15
  472.7 49.9 %all-gather.10.cloned.1.call-done = f32[32,128,128]{2,1,0:T(8,128)} async-done(((f32[4,128,128]{2,1,0:T(8,128)}), f32[32,128,128]{2,1,0:T(8,128)}) %all-gather.10.cloned.1.call-update) | async-done | bytes 2097168 | tf_op jit(solution)/shard_map/all_gather | solution.py:15
  522.7 20.3 %while.46 = (s32[]{:T(128)}, f32[4,128,128]{2,1,0:T(8,128)S(1)}, f32[4,128,128]{2,1,0:T(8,128)S(1)}, s32[]{:T(128)}, f32[8,4,128,128]{3,2,1,0:T(8,128)}, /*index...) while((s32[]{:T(128)}, f32[4,128,128]{2,1,0:T(8,128)S(1)}, f32[4,128,128]{2,1,0:T(8,128)S(1)}, ...), condition=%wide.region_7.8_spmd, body=%wide.region_6.7_spmd.sunk | while | flops 201392128 | bytes 2884747 | solution.py:23
  544.0 6.3 %bitcast_add_fusion = f32[4,2,8,128,128]{4,3,1,0,2:T(8,128)S(1)} fusion(f32[8,4,2,128,128]{4,3,2,1,0:T(8,128)} %get-tuple-element.128, f32[8,4,2,128,128]{4,3,2,1,0:T(8,128)} %get-tuple-element.119, f32[4,2,128,128]{3,2,0,1:T(8,128)S(1)} %convolution_add_fusion.3), kind=kOutput, calls=%fused_computation.40 | convolution fusion | flops 1611661312 | bytes 13107200 | tf_op jit(solution)/shard_map/hgpij,hgjk->hgpik/dot_general | solution.py:27
  550.4 3.9 fusion.59
  555.5 24.2 %all-gather.6.cloned.1.call-done = bf16[512,2048]{1,0:T(8,128)(2,1)} async-done(((bf16[512,512]{1,0:T(8,128)(2,1)}), bf16[512,2048]{1,0:T(8,128)(2,1)}) %all-gather.6.cloned.1.call-update) | async-done | bytes 2097168 | tf_op jit(solution)/shard_map/all_gather | solution.py:128
  579.7 4.3 fusion.56
  (135 shorter events, 82.7 us)
Async XLA Ops:
  6.5 536.4 %copy-start = (f32[4,128,128]{2,1,0:T(8,128)S(1)}, f32[4,128,128]{2,1,0:T(8,128)}, u32[]{:S(2)}) copy-start(f32[4,128,128]{2,1,0:T(8,128)} %param.14) | copy-start | bytes 786436
  6.5 466.1 %all-gather.8.cloned.1.call-start = ((), (), s32[]{:S(2)}) async-start(), calls=%async_computation.1 | async-start | bytes 2359296 | tf_op jit(solution)/shard_map/all_gather | solution.py:15
  9.3 1.3 copy-start.3
  10.7 2.2 copy-start.7
  14.9 3.2 copy-start.10
  345.1 6.8 %copy-start.1 = (f32[4,16,64,256]{3,2,1,0:T(8,128)}, f32[4,16,64,256]{3,2,1,0:T(8,128)S(1)}, u32[]{:S(2)}) copy-start(f32[4,16,64,256]{3,2,1,0:T(8,128)S(1)} %fusion.29) | copy-start | bytes 12582916
  418.3 1.3 copy-start.5
  421.7 1.3 copy-start.5
  424.1 0.7 copy-start.4
  424.8 97.8 %all-gather.10.cloned.1.call-start = ((), (), s32[]{:S(2)}) async-start(), calls=%async_computation.2 | async-start | bytes 2359296 | tf_op jit(solution)/shard_map/all_gather | solution.py:15
  425.6 154.1 %all-gather.6.cloned.1.call-start = ((), (), s32[]{:S(2)}) async-start(), calls=%async_computation | async-start | bytes 2621440 | tf_op jit(solution)/shard_map/all_gather | solution.py:128
  427.9 3.4 copy-start.2
  522.7 20.7 %copy-start.8 = (f32[2,4,128,128]{3,2,1,0:T(8,128)S(1)}, f32[2,4,128,128]{3,2,1,0:T(8,128)}, u32[]{:S(2)}) copy-start(f32[2,4,128,128]{3,2,1,0:T(8,128)} %get-tuple-element.122) | copy-start | bytes 1572868
  522.7 20.7 %copy-start.9 = (f32[2,4,128,128]{3,2,1,0:T(8,128)S(1)}, f32[2,4,128,128]{3,2,1,0:T(8,128)}, u32[]{:S(2)}) copy-start(f32[2,4,128,128]{3,2,1,0:T(8,128)} %get-tuple-element.127) | copy-start | bytes 1572868
  544.0 6.3 %copy-start.6 = (f32[4,16,32,128]{3,2,1,0:T(8,128)S(1)}, f32[4,16,32,128]{3,2,1,0:T(8,128)}, u32[]{:S(2)}) copy-start(f32[4,16,32,128]{3,2,1,0:T(8,128)} %fusion.43) | copy-start | bytes 3145732
Sparse Core Ops, SparseCore 0:
  425.0 47.6 all-gather.7
  474.8 47.7 all-gather.9
  555.6 23.9 all-gather.5
where the time goes:
time: 599 us; the launch traced here: 591 us
  other arithmetic  331 us (55%)
  waiting for transfers between devices  111 us (19%)
  matrix products  106 us (18%)
  local copies, waits for them, and re-layouts  28.6 us (5%)
  between operations  13.6 us (2%)
    another operation x4, other arithmetic, block_parts(): jax.scipy.linalg.solve_triangular(system, stacked, lower=True, unit_diago...  317 us
    dot_general x44, matrix products, product(): return jnp.einsum(pattern, left, right, precision=lax.Precision.HIGHEST)  95.3 us
    all_gather x2, waiting for transfers between devices, carried_in(): gathered = jax.tree.map(lambda a: lax.all_gather(a, axis), part)  86.1 us
    all_gather x1, waiting for transfers between devices, local(): lax.all_gather(attended, 'head', axis=1, tiled=True)  24.2 us
  transfers between devices with their start and end apart: 3, of which 3 were waited for; matrix products, arithmetic and copies ran while one was open for 2% of the time, Pallas kernels for 0%

commit v1 on v0

v1 whole, which is shorter than its diff:
```python
import functools

import jax
import jax.numpy as jnp
from jax import lax
from jax.experimental import pallas as pl
from jax.experimental.pallas import tpu as pltpu
from jax.sharding import PartitionSpec as P

WIDTH = 128
CHUNK = 64
MICRO = 2 * CHUNK
SMALL = 8
epsilon = 1e-06
f32, bf16 = jnp.float32, jnp.bfloat16


def dot(a, b, dims=((1,), (0,))):
    return lax.dot_general(a, b, (dims, ((), ())), preferred_element_type=f32)


def split(x):
    high = x.astype(bf16)
    return high, (x - high.astype(f32)).astype(bf16)


def wide_left(x):
    return jnp.concatenate(split(x), axis=1)


def wide_right(y):
    row = jnp.concatenate(split(y), axis=1)
    return jnp.concatenate([row, row], axis=0)


def exact_product(x, y):
    both = dot(wide_left(x), wide_right(y))
    half = y.shape[1]
    return both[:, :half] + both[:, half:]


def iota(shape, dim):
    return lax.broadcasted_iota(jnp.int32, shape, dim)


def small_inverse(lower):
    row, col = iota((MICRO, WIDTH), 0), iota((MICRO, WIDTH), 1)
    same = row // SMALL == col // SMALL
    packed = jnp.where(same, lower, 0.0).reshape(MICRO // SMALL, SMALL, WIDTH).sum(0)
    sub, lane = iota((SMALL, WIDTH), 0), iota((SMALL, WIDTH), 1)
    inverse = jnp.where(lane % SMALL == sub, 1.0, 0.0).astype(f32)
    for c in range(SMALL - 1):
        factor = jnp.take_along_axis(packed, lane // SMALL * SMALL + c, axis=1, mode="promise_in_bounds")
        inverse = inverse - factor * inverse[c : c + 1]
    return jnp.where(same, jnp.concatenate([inverse] * (MICRO // SMALL), axis=0), 0.0)


def odd_rows(x, b):
    return jnp.concatenate([x[i : i + b] for i in range(b, MICRO, 2 * b)], axis=0)


def weave(even, odd, b):
    rows = []
    for i in range(0, MICRO // 2, b):
        rows += [even[i : i + b], odd[i : i + b]]
    return jnp.concatenate(rows, axis=0)


def even_rows(x, b):
    return jnp.concatenate([x[i : i + b] for i in range(0, MICRO, 2 * b)], axis=0)


def unit_lower_inverses(lowers):
    inverses = [small_inverse(lower) for lower in lowers]
    half = MICRO // 2
    row, col = iota((half, WIDTH), 0), iota((half, WIDTH), 1)
    zeros = jnp.zeros((half, WIDTH), f32)
    b = SMALL
    while b < MICRO:
        below = col // b == row // b * 2
        firsts = [
            exact_product(jnp.where(below, odd_rows(lower, b), 0.0), inverse)
            for lower, inverse in zip(lowers, inverses)
        ]
        odds = [odd_rows(inverse, b) for inverse in inverses]
        seconds = [
            odd - exact_product(odd, weave(zeros, first, b)) for odd, first in zip(odds, firsts)
        ]
        inverses = [
            weave(even_rows(inverse, b), second, b) for inverse, second in zip(inverses, seconds)
        ]
        b *= 2
    return inverses


def chunk_kernel(heads, per_step, q_ref, k_ref, v_ref, a_ref, o_ref, map_ref, z_ref):
    step = pl.program_id(0)
    row, col = iota((MICRO, WIDTH), 0), iota((MICRO, WIDTH), 1)
    eye = jnp.where(row == col, 1.0, 0.0).astype(f32)

    @pl.when(step == 0)
    def _():
        for h in range(heads):
            z_ref[h] = jnp.concatenate([eye, jnp.zeros((WIDTH, WIDTH), f32)], axis=1)

    where = [(p, h) for p in range(per_step) for h in range(heads)]

    def key_of(p, h):
        return k_ref[p * MICRO : (p + 1) * MICRO, h * WIDTH : (h + 1) * WIDTH]

    lowers, scales = [], []
    for p, h in where:
        key = key_of(p, h)
        gram = dot(key, key, ((1,), (1,)))
        diagonal = jnp.where(row == col, gram, 0.0)
        down = lax.rsqrt(jnp.sum(diagonal, axis=1, keepdims=True) + epsilon)
        across = lax.rsqrt(jnp.sum(diagonal, axis=0, keepdims=True) + epsilon)
        lowers.append(jnp.where(row > col, 2.0 * gram * down * across, 0.0))
        scales.append((down, across))
    inverses = unit_lower_inverses(lowers)
    prepared = []
    for (p, h), inverse, (down, across) in zip(where, inverses, scales):
        key = key_of(p, h)
        value = v_ref[p * MICRO : (p + 1) * MICRO, h * WIDTH : (h + 1) * WIDTH]
        inverse = inverse * (2.0 * down)
        write_key = dot(wide_left(inverse * across), jnp.concatenate([key, key], axis=0))
        write_value = dot(wide_left(inverse), jnp.concatenate([value, value], axis=0))
        (wk_high, wk_low), (wv_high, wv_low) = split(write_key), split(write_value)
        effect = dot(
            key, jnp.concatenate([wk_high, wv_high, wk_low, wv_low], axis=1), ((0,), (0,))
        )
        effect = effect[:, : 2 * WIDTH] + effect[:, 2 * WIDTH :]
        move, carry = eye - effect[:, :WIDTH], effect[:, WIDTH:]
        query = q_ref[p * CHUNK : (p + 1) * CHUNK, h * WIDTH : (h + 1) * WIDTH]
        scores = dot(query, key, ((1,), (1,)))
        token, micro = iota((CHUNK, MICRO), 0), iota((CHUNK, MICRO), 1)
        scores = jnp.where(micro <= 2 * token + 1, scores, 0.0).astype(bf16)
        inner = dot(scores, jnp.concatenate([wk_high, wv_high], axis=1))
        query = query.astype(f32)
        size = lax.rsqrt(jnp.sum(query * query, axis=1, keepdims=True) + epsilon)
        adjusted = (query - inner[:, :WIDTH]) * size
        prepared.append((wide_left(move), carry, adjusted.astype(bf16), inner[:, WIDTH:] * size))
    for (p, h), (move, carry, adjusted, inside) in zip(where, prepared):
        state = z_ref[h]
        high, low = split(state)
        out = dot(adjusted, high)
        here = (slice(p * CHUNK, (p + 1) * CHUNK), slice(h * WIDTH, (h + 1) * WIDTH))
        a_ref[here] = out[:, :WIDTH].astype(bf16)
        o_ref[here] = (out[:, WIDTH:] + inside).astype(o_ref.dtype)
        both = jnp.concatenate([high, low], axis=1)
        moved = dot(move, jnp.concatenate([both, both], axis=0))
        moved = moved[:, : 2 * WIDTH] + moved[:, 2 * WIDTH :]
        z_ref[h] = jnp.concatenate([moved[:, :WIDTH], moved[:, WIDTH:] + carry], axis=1)

    @pl.when(step == pl.num_programs(0) - 1)
    def _():
        map_ref[...] = z_ref[...].astype(map_ref.dtype)


def chunk_maps(queries, keys, values, wire):
    tokens, width = queries.shape
    heads = width // WIDTH
    per_step = 2
    rows = per_step * CHUNK
    return pl.pallas_call(
        functools.partial(chunk_kernel, heads, per_step),
        grid=(tokens // rows,),
        in_specs=[
            pl.BlockSpec((rows, width), lambda i: (i, 0)),
            pl.BlockSpec((2 * rows, width), lambda i: (i, 0)),
            pl.BlockSpec((2 * rows, width), lambda i: (i, 0)),
        ],
        out_specs=[
            pl.BlockSpec((rows, width), lambda i: (i, 0)),
            pl.BlockSpec((rows, width), lambda i: (i, 0)),
            pl.BlockSpec((heads, WIDTH, 2 * WIDTH), lambda i: (0, 0, 0)),
        ],
        out_shape=[
            jax.ShapeDtypeStruct((tokens, width), bf16),
            jax.ShapeDtypeStruct((tokens, width), f32),
            jax.ShapeDtypeStruct((heads, WIDTH, 2 * WIDTH), wire),
        ],
        scratch_shapes=[pltpu.VMEM((heads, WIDTH, 2 * WIDTH), f32)],
        compiler_params=pltpu.CompilerParams(vmem_limit_bytes=40 * 2**20),
        name="chunk_maps",
    )(queries, keys, values)


def enter_kernel(heads, place_ref, maps_ref, init_ref, a_ref, o_ref, out_ref, s_ref):
    s_ref[...] = init_ref[...]

    def one(j, _):
        for h in range(heads):
            parts = maps_ref[j, h]
            state = jnp.concatenate(split(s_ref[h]), axis=1)
            if parts.dtype == bf16:
                moved = dot(parts[:, :WIDTH], state)
            else:
                moved = dot(wide_left(parts[:, :WIDTH]), jnp.concatenate([state, state], axis=0))
            s_ref[h] = moved[:, :WIDTH] + moved[:, WIDTH:] + parts[:, WIDTH:].astype(f32)
        return 0

    lax.fori_loop(0, place_ref[0], one, 0)
    for h in range(heads):
        cols = slice(h * WIDTH, (h + 1) * WIDTH)
        out_ref[:, cols] = (dot(a_ref[:, cols], s_ref[h].astype(bf16)) + o_ref[:, cols]).astype(bf16)


def enter(maps, init_state, a, o):
    heads = init_state.shape[0]
    vmem = pl.BlockSpec(memory_space=pltpu.VMEM)
    return pl.pallas_call(
        functools.partial(enter_kernel, heads),
        in_specs=[pl.BlockSpec(memory_space=pltpu.SMEM)] + [vmem] * 4,
        out_specs=vmem,
        out_shape=jax.ShapeDtypeStruct(a.shape, bf16),
        scratch_shapes=[pltpu.VMEM(init_state.shape, f32)],
        compiler_params=pltpu.CompilerParams(vmem_limit_bytes=40 * 2**20),
        name="enter",
    )(lax.axis_index("seq").reshape(1).astype(jnp.int32), maps, init_state, a, o)


def local(queries, key_pairs, value_pairs, init_state, out_weight):
    tokens, width = queries.shape
    wire = bf16 if lax.axis_size("seq") <= 8 else f32
    keys = key_pairs.reshape(2 * tokens, width)
    values = value_pairs.reshape(2 * tokens, width)
    a, o, maps = chunk_maps(queries, keys, values, wire)
    attended = enter(lax.all_gather(maps, "seq"), init_state, a, o)
    model_cols = out_weight.shape[1] // lax.axis_size("head")
    own_cols = lax.dynamic_slice_in_dim(
        out_weight, lax.axis_index("head") * model_cols, model_cols, 1
    )
    return jnp.dot(
        lax.all_gather(attended, "head", axis=1, tiled=True),
        own_cols,
        preferred_element_type=jnp.float32,
    ).astype(jnp.bfloat16)


def solution(mesh):
    in_specs = (
        P("seq", "head"),
        P("seq", None, "head"),
        P("seq", None, "head"),
        P("head", None, None),
        P(),
    )
    out_specs = P("seq", "head")
    return jax.shard_map(local, mesh=mesh, in_specs=in_specs, out_specs=out_specs, check_vma=False)
```

time: 599 us -> 120 us (0.20); the launches traced: 591 us -> 119 us
  other arithmetic: 331 us -> 0 us
  matrix products: 106 us -> 4.26 us
  waiting for transfers between devices: 111 us -> 72 us
  Pallas kernels: 0 us -> 21.7 us
  local copies, waits for them, and re-layouts: 28.6 us -> 7.15 us
    another operation x8 -> x0, other arithmetic: 317 us -> none  [the longest x4 317 us: block_parts(): jax.scipy.linalg.solve_triangular(system, stacked, lower=True, unit_diago...]
    dot_general x44 -> x0, matrix products: 95.3 us -> none  [product(): return jnp.einsum(pattern, left, right, precision=lax.Precision.HIGHEST)]
    all_gather x2 -> x1, waiting for transfers between devices: 86.1 us -> 47.8 us  [local(): attended = enter(lax.all_gather(maps, 'seq'), init_state, a, o)]
    pallas_call x0 -> x2, Pallas kernels: none -> 21.7 us  [the longest x1 19.1 us: chunk_maps(): pl.pallas_call(functools.partial(chunk_kernel, heads, per_step), grid=(to...]
    while x40 -> x0, local copies, waits for them, and re-layouts: 12.7 us -> none
    dynamic_update_slice x10 -> x0, other arithmetic: 10.5 us -> none  [the longest x8 8.72 us: local(): lax.scan(advance_map, (group_identity, group_zeros), (grouped(moving), gr...]
    convert_element_type x5 -> x0, local copies, waits for them, and re-layouts: 8.94 us -> none  [the longest x2 5.17 us: block_parts(): value_block = value_block.astype(jnp.float32)]
    another operation x1 -> x0, matrix products: 6.12 us -> none  [block_parts(): jax.scipy.linalg.solve_triangular(system, stacked, lower=True, unit_diago...]
  transfers between devices with their start and end apart: 3 -> 2, of which waited for: 3 -> 2; matrix products, arithmetic and copies ran while one was open for 2% -> 0% of each run, Pallas kernels for 0% -> 0%
where the time goes in v1:
time: 120 us; the launch traced here: 119 us
  waiting for transfers between devices  72 us (60%)
  Pallas kernels  21.7 us (18%)
  between operations  13.5 us (11%)
  local copies, waits for them, and re-layouts  7.15 us (6%)
  matrix products  4.26 us (4%)
    all_gather x1, waiting for transfers between devices, local(): attended = enter(lax.all_gather(maps, 'seq'), init_state, a, o)  47.8 us
    all_gather x1, waiting for transfers between devices, local(): lax.all_gather(attended, 'head', axis=1, tiled=True)  24.2 us
    pallas_call x1, Pallas kernels, chunk_maps(): pl.pallas_call(functools.partial(chunk_kernel, heads, per_step), grid=(to...  19.1 us
    unnamed x14, local copies, waits for them, and re-layouts  5.16 us
    dot_general x1, matrix products, local(): jnp.dot(lax.all_gather(attended, 'head', axis=1, tiled=True), own_cols, p...  4.26 us
    pallas_call x1, Pallas kernels, enter(): pl.pallas_call(functools.partial(enter_kernel, heads), in_specs=[pl.Block...  2.65 us
  transfers between devices with their start and end apart: 2, of which 2 were waited for; matrix products, arithmetic and copies ran while one was open for 0% of the time, Pallas kernels for 0%

profile of v1, /device:TPU:29, one launch (start us, length us, event | category | flops | bytes accessed | tf_op | source)
XLA Modules:
  0.0 118.6 jit_solution(1961841068145093894)
XLA Ops:
  6.5 0.0 copy-start.6
  6.5 0.0 all-gather.6.cloned.1.call-start
  6.5 1.6 %reshape.10.k_ref = bf16[1024,512]{1,0:T(8,128)(2,1)S(1)} reshape(bf16[512,2,512]{2,1,0:T(2,128)(2,1)} %param.6) | data formatting | bytes 2097152 | tf_op jit(solution)/shard_map/reshape | solution.py:226
  8.1 0.0 copy-done.6
  8.1 0.0 copy-start.4
  8.1 0.4 reshape.11.v_ref
  8.6 0.0 copy-start.1
  8.6 1.0 copy-done.1
  9.6 19.1 %chunk_maps.1 = (bf16[512,512]{1,0:T(8,128)(2,1)S(1)}, f32[512,512]{1,0:T(8,128)S(1)}, bf16[4,128,256]{2,1,0:T(8,128)(2,1)S(1)}) custom-call(bf16[512,512]{1,0:T(8,128)(2,1)S(1)} %copy-done.1, bf16[1024,512]{1,0:T(8,128)(2,1)S(1)} %reshape.10.k_ref, bf16[1024,512]{1,0:T(8,128)(2,1)S(1)} %reshape.11.v_ref), custom_call_target="tpu_custom_call" | custom-call | tf_op jit(solution)/shard_map/chunk_maps/pallas_call | solution.py:165
  28.7 0.0 copy-start.2
  28.7 0.8 copy-done.2
  29.5 0.0 copy-start.5
  29.5 0.7 copy-done.5
  30.2 0.0 all-gather.6.cloned.1.call-update
  30.2 0.0 all-gather.4.cloned.1.call-start
  30.3 47.8 %all-gather.6.cloned.1.call-done = bf16[32,128,256]{2,1,0:T(8,128)(2,1)} async-done(((bf16[4,128,256]{2,1,0:T(8,128)(2,1)}), bf16[32,128,256]{2,1,0:T(8,128)(2,1)}) %all-gather.6.cloned.1.call-update) | async-done | bytes 2097168 | tf_op jit(solution)/shard_map/all_gather | solution.py:229
  78.1 0.0 copy-done.4
  78.1 0.0 copy-start
  78.1 1.6 %copy-done = bf16[32,128,256]{2,1,0:T(8,128)(2,1)S(1)} copy-done((bf16[32,128,256]{2,1,0:T(8,128)(2,1)S(1)}, bf16[32,128,256]{2,1,0:T(8,128)(2,1)}, u32[]{:S(2)}) %copy-start) | copy-done | bytes 2097176
  79.7 1.0 copy-done.3
  80.7 2.6 %enter.1 = bf16[512,512]{1,0:T(8,128)(2,1)} custom-call(s32[1]{0:T(128)} %bitcast.place_ref, bf16[8,4,128,256]{3,2,1,0:T(8,128)(2,1)S(1)} %bitcast.3, f32[4,128,128]{2,1,0:T(8,128)S(1)} %copy-done.4, bf16[512,512]{1,0:T(8,128)(2,1)S(1)} %copy-done.3, f32[512,512]{1,0:T(8,128)S(1)} %get-tuple-element.10.o_ref), custom_call_target="tpu_custom_call" | custom-call | tf_op jit(solution)/shard_map/enter/pallas_call | solution.py:212
  83.3 0.0 all-gather.4.cloned.1.call-update
  83.4 24.2 %all-gather.4.cloned.1.call-done = bf16[512,2048]{1,0:T(8,128)(2,1)} async-done(((bf16[512,512]{1,0:T(8,128)(2,1)}), bf16[512,2048]{1,0:T(8,128)(2,1)}) %all-gather.4.cloned.1.call-update) | async-done | bytes 2097168 | tf_op jit(solution)/shard_map/all_gather | solution.py:235
  107.5 4.3 %fusion.2 = bf16[512,512]{1,0:T(8,128)(2,1)} fusion(bf16[512,2048]{1,0:T(8,128)(2,1)} %all-gather.4.cloned.1.call-done, bf16[2048,2048]{1,0:T(8,128)(2,1)} %param.9, s32[]{:T(128)S(6)} %select_n.3), kind=kOutput, calls=%fused_computation.2 | convolution fusion | flops 1074003968 | bytes 4718596 | tf_op jit(solution)/shard_map/dot_general | solution.py:234
  (1 shorter events, 0.0 us)
Async XLA Ops:
  6.5 1.6 %copy-start.6 = (bf16[512,2,512]{2,1,0:T(2,128)(2,1)S(1)}, bf16[512,2,512]{2,1,0:T(2,128)(2,1)}, u32[]{:S(2)}) copy-start(bf16[512,2,512]{2,1,0:T(2,128)(2,1)} %param.7) | copy-start | bytes 3145732
  6.5 71.5 %all-gather.6.cloned.1.call-start = ((), (), s32[]{:S(2)}) async-start(), calls=%async_computation.1 | async-start | bytes 2359296 | tf_op jit(solution)/shard_map/all_gather | solution.py:229
  8.1 70.0 %copy-start.4 = (f32[4,128,128]{2,1,0:T(8,128)S(1)}, f32[4,128,128]{2,1,0:T(8,128)}, u32[]{:S(2)}) copy-start(f32[4,128,128]{2,1,0:T(8,128)} %init_ref.1) | copy-start | bytes 786436
  8.6 1.0 copy-start.1
  28.7 0.8 copy-start.2
  29.5 0.7 copy-start.5
  30.2 77.3 %all-gather.4.cloned.1.call-start = ((), (), s32[]{:S(2)}) async-start(), calls=%async_computation | async-start | bytes 2621440 | tf_op jit(solution)/shard_map/all_gather | solution.py:235
  78.1 1.6 %copy-start = (bf16[32,128,256]{2,1,0:T(8,128)(2,1)S(1)}, bf16[32,128,256]{2,1,0:T(8,128)(2,1)}, u32[]{:S(2)}) copy-start(bf16[32,128,256]{2,1,0:T(8,128)(2,1)} %all-gather.6.cloned.1.call-done) | copy-start | bytes 6291460
  79.7 1.0 copy-start.3
Sparse Core Ops, SparseCore 0:
  30.4 47.6 all-gather.5
  83.5 23.9 all-gather.3

commit v2 on v1

--- a/solution.py
+++ b/solution.py
@@ -186,38 +186,149 @@
     )(queries, keys, values)
 
 
-def enter_kernel(heads, place_ref, maps_ref, init_ref, a_ref, o_ref, out_ref, s_ref):
-    s_ref[...] = init_ref[...]
-
-    def one(j, _):
-        for h in range(heads):
-            parts = maps_ref[j, h]
-            state = jnp.concatenate(split(s_ref[h]), axis=1)
-            if parts.dtype == bf16:
-                moved = dot(parts[:, :WIDTH], state)
-            else:
-                moved = dot(wide_left(parts[:, :WIDTH]), jnp.concatenate([state, state], axis=0))
-            s_ref[h] = moved[:, :WIDTH] + moved[:, WIDTH:] + parts[:, WIDTH:].astype(f32)
-        return 0
-
-    lax.fori_loop(0, place_ref[0], one, 0)
+def finish_kernel(
+    shards, heads, maps_ref, init_ref, a_ref, o_ref, w_hbm, out_ref,
+    w_ref, move_ref, state_ref, wire_out, wire_in, att_ref, acc_ref,
+    w_sem, chain_send, chain_recv, att_send, att_recv,
+):
+    place, group = lax.axis_index("seq"), lax.axis_index("head")
+    across = lax.rem(group + 2, 4)
+    beside = group + 1 - 2 * lax.rem(group, 2)
+    beyond = lax.rem(beside + 2, 4)
+    depth, cols = heads * WIDTH, out_ref.shape[1]
+    w_copy = pltpu.make_async_copy(
+        w_hbm.at[:, pl.ds(pl.multiple_of(group * cols, cols), cols)], w_ref, w_sem
+    )
+    w_copy.start()
+
+    barrier = pltpu.get_barrier_semaphore()
+
+    def greet(target):
+        pl.semaphore_signal(barrier, inc=1, device_id=target, device_id_type=pl.DeviceIdType.MESH)
+
+    greet((place, across))
+    greet((place, beside))
+
+    @pl.when(place > 0)
+    def _():
+        greet((place - 1, group))
+
+    @pl.when(place < shards - 1)
+    def _():
+        greet((place + 1, group))
+
     for h in range(heads):
-        cols = slice(h * WIDTH, (h + 1) * WIDTH)
-        out_ref[:, cols] = (dot(a_ref[:, cols], s_ref[h].astype(bf16)) + o_ref[:, cols]).astype(bf16)
-
-
-def enter(maps, init_state, a, o):
+        move_ref[h] = wide_left(maps_ref[h, :, :WIDTH])
+
+    ends = jnp.where(place == 0, 1, 0) + jnp.where(place == shards - 1, 1, 0)
+    pl.semaphore_wait(barrier, 4 - ends)
+
+    def chain(h):
+        return pltpu.make_async_remote_copy(
+            src_ref=wire_out.at[h], dst_ref=wire_in.at[h],
+            send_sem=chain_send.at[h], recv_sem=chain_recv.at[h],
+            device_id=(place + 1, group), device_id_type=pl.DeviceIdType.MESH,
+        )
+
+    def pass_on(source, slot, h, target):
+        return pltpu.make_async_remote_copy(
+            src_ref=att_ref.at[source, h], dst_ref=att_ref.at[slot, h],
+            send_sem=att_send.at[slot, h], recv_sem=att_recv.at[slot, h],
+            device_id=(place, target), device_id_type=pl.DeviceIdType.MESH,
+        )
+
+    to_across = [pass_on(0, 1, h, across) for h in range(heads)]
+    to_beside = [pass_on(0, 2, h, beside) for h in range(heads)]
+    relayed = [pass_on(1, 3, h, beside) for h in range(heads)]
+
+    for h in range(heads):
+
+        @pl.when(place == 0)
+        def _():
+            state_ref[h] = init_ref[h]
+
+        @pl.when(place > 0)
+        def _():
+            chain(h).wait_recv()
+            state_ref[h] = wire_in[h].astype(f32)
+
+        @pl.when(place < shards - 1)
+        def _():
+            both = jnp.concatenate(split(state_ref[h]), axis=1)
+            moved = dot(move_ref[h], jnp.concatenate([both, both], axis=0))
+            moved = moved[:, :WIDTH] + moved[:, WIDTH:] + maps_ref[h, :, WIDTH:]
+            wire_out[h] = moved.astype(wire_out.dtype)
+            chain(h).start()
+
+        here = slice(h * WIDTH, (h + 1) * WIDTH)
+        att_ref[0, h] = (
+            dot(a_ref[:, here], state_ref[h].astype(bf16)) + o_ref[:, here]
+        ).astype(bf16)
+        to_across[h].start()
+        to_beside[h].start()
+
+    w_copy.wait()
+
+    def project(slot, owner, first, count):
+        rows = pl.multiple_of(owner * depth, depth) + first * WIDTH
+        left = jnp.concatenate([att_ref[slot, first + i] for i in range(count)], axis=1)
+        return dot(left, w_ref[pl.ds(pl.multiple_of(rows, WIDTH), count * WIDTH), :])
+
+    acc_ref[...] = project(0, group, 0, heads)
+    for h in range(heads):
+        to_across[h].wait_recv()
+        relayed[h].start()
+        if h == 0:
+            for i in range(heads):
+                to_beside[i].wait_recv()
+            acc_ref[...] += project(2, beside, 0, heads)
+        if h % 2 == 1:
+            acc_ref[...] += project(1, across, h - 1, 2)
+            if h > 1:
+                relayed[h - 3].wait_recv()
+                relayed[h - 2].wait_recv()
+                acc_ref[...] += project(3, beyond, h - 3, 2)
+    relayed[heads - 2].wait_recv()
+    relayed[heads - 1].wait_recv()
+    out_ref[...] = (acc_ref[...] + project(3, beyond, heads - 2, 2)).astype(bf16)
+    for h in range(heads):
+        to_across[h].wait_send()
+        to_beside[h].wait_send()
+        relayed[h].wait_send()
+
+        @pl.when(place < shards - 1)
+        def _():
+            chain(h).wait_send()
+
+
+def finish(maps, init_state, a, o, out_weight, wire):
     heads = init_state.shape[0]
+    shards = lax.axis_size("seq")
+    tokens = a.shape[0]
+    features = out_weight.shape[0]
+    cols = out_weight.shape[1] // lax.axis_size("head")
     vmem = pl.BlockSpec(memory_space=pltpu.VMEM)
+    dma = pltpu.SemaphoreType.DMA
     return pl.pallas_call(
-        functools.partial(enter_kernel, heads),
-        in_specs=[pl.BlockSpec(memory_space=pltpu.SMEM)] + [vmem] * 4,
+        functools.partial(finish_kernel, shards, heads),
+        in_specs=[vmem] * 4 + [pl.BlockSpec(memory_space=pl.ANY)],
         out_specs=vmem,
-        out_shape=jax.ShapeDtypeStruct(a.shape, bf16),
-        scratch_shapes=[pltpu.VMEM(init_state.shape, f32)],
-        compiler_params=pltpu.CompilerParams(vmem_limit_bytes=40 * 2**20),
-        name="enter",
-    )(lax.axis_index("seq").reshape(1).astype(jnp.int32), maps, init_state, a, o)
+        out_shape=jax.ShapeDtypeStruct((tokens, cols), bf16),
+        scratch_shapes=[
+            pltpu.VMEM((features, cols), bf16),
+            pltpu.VMEM((heads, WIDTH, 2 * WIDTH), bf16),
+            pltpu.VMEM((heads, WIDTH, WIDTH), f32),
+            pltpu.VMEM((heads, WIDTH, WIDTH), wire),
+            pltpu.VMEM((heads, WIDTH, WIDTH), wire),
+            pltpu.VMEM((4, heads, tokens, WIDTH), bf16),
+            pltpu.VMEM((tokens, cols), f32),
+            dma, dma((heads,)), dma((heads,)), dma((4, heads)), dma((4, heads)),
+        ],
+        compiler_params=pltpu.CompilerParams(
+            vmem_limit_bytes=40 * 2**20, collective_id=0, has_side_effects=True
+        ),
+        name="finish",
+    )(maps, init_state, a, o, out_weight)
 
 
 def local(queries, key_pairs, value_pairs, init_state, out_weight):
@@ -225,17 +336,8 @@
     wire = bf16 if lax.axis_size("seq") <= 8 else f32
     keys = key_pairs.reshape(2 * tokens, width)
     values = value_pairs.reshape(2 * tokens, width)
-    a, o, maps = chunk_maps(queries, keys, values, wire)
-    attended = enter(lax.all_gather(maps, "seq"), init_state, a, o)
-    model_cols = out_weight.shape[1] // lax.axis_size("head")
-    own_cols = lax.dynamic_slice_in_dim(
-        out_weight, lax.axis_index("head") * model_cols, model_cols, 1
-    )
-    return jnp.dot(
-        lax.all_gather(attended, "head", axis=1, tiled=True),
-        own_cols,
-        preferred_element_type=jnp.float32,
-    ).astype(jnp.bfloat16)
+    a, o, maps = chunk_maps(queries, keys, values, f32)
+    return finish(maps, init_state, a, o, out_weight, wire)
 
 
 def solution(mesh):

time: 120 us -> 62.4 us (0.52)
  waiting for transfers between devices: 72 us -> 0 us
  Pallas kernels: 21.7 us -> 53 us
  between operations: 13.5 us -> 0.05 us
  matrix products: 4.26 us -> 0 us
  local copies, waits for them, and re-layouts: 7.15 us -> 9.09 us
    all_gather x2 -> x0, waiting for transfers between devices: 71.9 us -> none  [the longest x1 47.8 us: local(): attended = enter(lax.all_gather(maps, 'seq'), init_state, a, o)]
    pallas_call x1, Pallas kernels: 2.65 us -> 33.9 us  [finish(): pl.pallas_call(functools.partial(finish_kernel, shards, heads), in_specs=...]
    dot_general x1 -> x0, matrix products: 4.26 us -> none  [local(): jnp.dot(lax.all_gather(attended, 'head', axis=1, tiled=True), own_cols, p...]
    unnamed x14 -> x7, local copies, waits for them, and re-layouts: 5.16 us -> 6.16 us
  transfers between devices with their start and end apart: 2 -> 0, of which waited for: 2 -> 0; matrix products, arithmetic and copies ran while one was open for 0% -> 0% of each run, Pallas kernels for 0% -> 0%
where the time goes in v2:
time: 62.4 us; the launch traced here: 62.1 us
  Pallas kernels  53 us (85%)
  local copies, waits for them, and re-layouts  9.09 us (15%)
    pallas_call x1, Pallas kernels, finish(): pl.pallas_call(functools.partial(finish_kernel, shards, heads), in_specs=...  33.9 us
    pallas_call x1, Pallas kernels, chunk_maps(): pl.pallas_call(functools.partial(chunk_kernel, heads, per_step), grid=(to...  19.1 us
    unnamed x7, local copies, waits for them, and re-layouts  6.16 us
    reshape x1, local copies, waits for them, and re-layouts, local(): values = value_pairs.reshape(2 * tokens, width)  1.47 us
    reshape x1, local copies, waits for them, and re-layouts, local(): keys = key_pairs.reshape(2 * tokens, width)  1.47 us

profile of v2, /device:TPU:29, one launch (start us, length us, event | category | flops | bytes accessed | tf_op | source)
XLA Modules:
  0.0 62.1 jit_solution(12867581864157469858)
XLA Ops:
  0.0 1.5 %reshape.6.k_ref = bf16[1024,512]{1,0:T(8,128)(2,1)S(1)} reshape(bf16[512,2,512]{2,1,0:T(2,128)(2,1)} %param.6) | data formatting | bytes 2097152 | tf_op jit(solution)/shard_map/reshape | solution.py:337
  1.5 1.5 %reshape.7.v_ref = bf16[1024,512]{1,0:T(8,128)(2,1)S(1)} reshape(bf16[512,2,512]{2,1,0:T(2,128)(2,1)} %param.7) | data formatting | bytes 2097152 | tf_op jit(solution)/shard_map/reshape | solution.py:338
  3.0 0.0 copy-start.1
  3.0 1.0 %copy-done.1 = bf16[512,512]{1,0:T(8,128)(2,1)S(1)} copy-done((bf16[512,512]{1,0:T(8,128)(2,1)S(1)}, bf16[512,512]{1,0:T(8,128)(2,1)}, u32[]{:S(2)}) %copy-start.1) | copy-done | bytes 524312
  4.0 19.1 %chunk_maps.1 = (bf16[512,512]{1,0:T(8,128)(2,1)S(1)}, f32[512,512]{1,0:T(8,128)S(1)}, f32[4,128,256]{2,1,0:T(8,128)S(1)}) custom-call(bf16[512,512]{1,0:T(8,128)(2,1)S(1)} %copy-done.1, bf16[1024,512]{1,0:T(8,128)(2,1)S(1)} %reshape.6.k_ref, bf16[1024,512]{1,0:T(8,128)(2,1)S(1)} %reshape.7.v_ref), custom_call_target="tpu_custom_call" | custom-call | tf_op jit(solution)/shard_map/chunk_maps/pallas_call | solution.py:165
  23.1 0.0 copy-start
  23.1 3.4 %copy-done = bf16[2048,2048]{1,0:T(8,128)(2,1)S(1)} copy-done((bf16[2048,2048]{1,0:T(8,128)(2,1)S(1)}, bf16[2048,2048]{1,0:T(8,128)(2,1)}, u32[]{:S(2)}) %copy-start) | copy-done | bytes 8388632
  26.5 0.0 copy-start.2
  26.5 0.9 %copy-done.2 = f32[4,128,128]{2,1,0:T(8,128)S(1)} copy-done((f32[4,128,128]{2,1,0:T(8,128)S(1)}, f32[4,128,128]{2,1,0:T(8,128)}, u32[]{:S(2)}) %copy-start.2) | copy-done | bytes 262168
  27.4 33.9 %finish.1 = bf16[512,512]{1,0:T(8,128)(2,1)S(1)} custom-call(f32[4,128,256]{2,1,0:T(8,128)S(1)} %get-tuple-element.8.maps_ref, f32[4,128,128]{2,1,0:T(8,128)S(1)} %copy-done.2, bf16[512,512]{1,0:T(8,128)(2,1)S(1)} %get-tuple-element.9.a_ref, f32[512,512]{1,0:T(8,128)S(1)} %get-tuple-element.10.o_ref, bf16[2048,2048]{1,0:T(8,128)(2,1)S(1)} %copy-done), custom_call_target="tpu_custom_call" | custom-call | tf_op jit(solution)/shard_map/finish/pallas_call | solution.py:312
  61.3 0.8 %copy.7 = bf16[512,512]{1,0:T(8,128)(2,1)} copy(bf16[512,512]{1,0:T(8,128)(2,1)S(1)} %finish.1) | data formatting | bytes 1048576
Async XLA Ops:
  3.0 1.0 %copy-start.1 = (bf16[512,512]{1,0:T(8,128)(2,1)S(1)}, bf16[512,512]{1,0:T(8,128)(2,1)}, u32[]{:S(2)}) copy-start(bf16[512,512]{1,0:T(8,128)(2,1)} %q_ref.1) | copy-start | bytes 1572868
  23.1 3.4 %copy-start = (bf16[2048,2048]{1,0:T(8,128)(2,1)S(1)}, bf16[2048,2048]{1,0:T(8,128)(2,1)}, u32[]{:S(2)}) copy-start(bf16[2048,2048]{1,0:T(8,128)(2,1)} %w_hbm.1) | copy-start | bytes 25165828
  26.5 0.9 %copy-start.2 = (f32[4,128,128]{2,1,0:T(8,128)S(1)}, f32[4,128,128]{2,1,0:T(8,128)}, u32[]{:S(2)}) copy-start(f32[4,128,128]{2,1,0:T(8,128)} %init_ref.1) | copy-start | bytes 786436

commit v3 on v2

--- a/solution.py
+++ b/solution.py
@@ -93,6 +93,11 @@
     return inverses
 
 
+def pair_rows(ref, p, h):
+    pairs = ref[p * CHUNK : (p + 1) * CHUNK, :, h * WIDTH : (h + 1) * WIDTH]
+    return pairs.reshape(MICRO, WIDTH)
+
+
 def chunk_kernel(heads, per_step, q_ref, k_ref, v_ref, a_ref, o_ref, map_ref, z_ref):
     step = pl.program_id(0)
     row, col = iota((MICRO, WIDTH), 0), iota((MICRO, WIDTH), 1)
@@ -106,7 +111,7 @@
     where = [(p, h) for p in range(per_step) for h in range(heads)]
 
     def key_of(p, h):
-        return k_ref[p * MICRO : (p + 1) * MICRO, h * WIDTH : (h + 1) * WIDTH]
+        return pair_rows(k_ref, p, h)
 
     lowers, scales = [], []
     for p, h in where:
@@ -121,7 +126,7 @@
     prepared = []
     for (p, h), inverse, (down, across) in zip(where, inverses, scales):
         key = key_of(p, h)
-        value = v_ref[p * MICRO : (p + 1) * MICRO, h * WIDTH : (h + 1) * WIDTH]
+        value = pair_rows(v_ref, p, h)
         inverse = inverse * (2.0 * down)
         write_key = dot(wide_left(inverse * across), jnp.concatenate([key, key], axis=0))
         write_value = dot(wide_left(inverse), jnp.concatenate([value, value], axis=0))
@@ -167,8 +172,8 @@
         grid=(tokens // rows,),
         in_specs=[
             pl.BlockSpec((rows, width), lambda i: (i, 0)),
-            pl.BlockSpec((2 * rows, width), lambda i: (i, 0)),
-            pl.BlockSpec((2 * rows, width), lambda i: (i, 0)),
+            pl.BlockSpec((rows, 2, width), lambda i: (i, 0, 0)),
+            pl.BlockSpec((rows, 2, width), lambda i: (i, 0, 0)),
         ],
         out_specs=[
             pl.BlockSpec((rows, width), lambda i: (i, 0)),
@@ -181,7 +186,7 @@
             jax.ShapeDtypeStruct((heads, WIDTH, 2 * WIDTH), wire),
         ],
         scratch_shapes=[pltpu.VMEM((heads, WIDTH, 2 * WIDTH), f32)],
-        compiler_params=pltpu.CompilerParams(vmem_limit_bytes=40 * 2**20),
+        compiler_params=pltpu.CompilerParams(vmem_limit_bytes=56 * 2**20),
         name="chunk_maps",
     )(queries, keys, values)
 
@@ -325,18 +330,15 @@
             dma, dma((heads,)), dma((heads,)), dma((4, heads)), dma((4, heads)),
         ],
         compiler_params=pltpu.CompilerParams(
-            vmem_limit_bytes=40 * 2**20, collective_id=0, has_side_effects=True
+            vmem_limit_bytes=56 * 2**20, collective_id=0, has_side_effects=True
         ),
         name="finish",
     )(maps, init_state, a, o, out_weight)
 
 
 def local(queries, key_pairs, value_pairs, init_state, out_weight):
-    tokens, width = queries.shape
     wire = bf16 if lax.axis_size("seq") <= 8 else f32
-    keys = key_pairs.reshape(2 * tokens, width)
-    values = value_pairs.reshape(2 * tokens, width)
-    a, o, maps = chunk_maps(queries, keys, values, f32)
+    a, o, maps = chunk_maps(queries, key_pairs, value_pairs, f32)
     return finish(maps, init_state, a, o, out_weight, wire)
 
 

time: 62.4 us -> 59.2 us (0.949)
  local copies, waits for them, and re-layouts: 9.09 us -> 1.87 us
  Pallas kernels: 53 us -> 57.1 us
    unnamed x7 -> x1, local copies, waits for them, and re-layouts: 6.16 us -> 1.87 us
    reshape x2 -> x0, local copies, waits for them, and re-layouts: 2.94 us -> none  [the longest x1 1.47 us: local(): values = value_pairs.reshape(2 * tokens, width)]
    pallas_call x1, Pallas kernels: 33.9 us -> 36 us  [finish(): pl.pallas_call(functools.partial(finish_kernel, shards, heads), in_specs=...]
    pallas_call x1, Pallas kernels: 19.1 us -> 21.1 us  [chunk_maps(): pl.pallas_call(functools.partial(chunk_kernel, heads, per_step), grid=(to...]
where the time goes in v3:
time: 59.2 us; the launch traced here: 59 us
  Pallas kernels  57.1 us (96%)
  local copies, waits for them, and re-layouts  1.87 us (3%)
    pallas_call x1, Pallas kernels, finish(): pl.pallas_call(functools.partial(finish_kernel, shards, heads), in_specs=...  36 us
    pallas_call x1, Pallas kernels, chunk_maps(): pl.pallas_call(functools.partial(chunk_kernel, heads, per_step), grid=(to...  21.1 us
    unnamed x1, local copies, waits for them, and re-layouts  1.87 us

profile of v3, /device:TPU:29, one launch (start us, length us, event | category | flops | bytes accessed | tf_op | source)
XLA Modules:
  0.0 59.0 jit_solution(10630874352421218441)
XLA Ops:
  0.0 21.1 %chunk_maps.1 = (bf16[512,512]{1,0:T(8,128)(2,1)}, f32[512,512]{1,0:T(8,128)}, f32[4,128,256]{2,1,0:T(8,128)}) custom-call(bf16[512,512]{1,0:T(8,128)(2,1)} %q_ref.1, bf16[512,2,512]{2,1,0:T(2,128)(2,1)} %k_ref.1, bf16[512,2,512]{2,1,0:T(2,128)(2,1)} %v_ref.1), custom_call_target="tpu_custom_call" | custom-call | tf_op jit(solution)/shard_map/chunk_maps/pallas_call | solution.py:170
  21.1 36.0 %finish.1 = bf16[512,512]{1,0:T(8,128)(2,1)} custom-call(f32[4,128,256]{2,1,0:T(8,128)} %get-tuple-element.8.maps_ref, f32[4,128,128]{2,1,0:T(8,128)} %init_ref.1, bf16[512,512]{1,0:T(8,128)(2,1)} %get-tuple-element.9.a_ref, f32[512,512]{1,0:T(8,128)} %get-tuple-element.10.o_ref, bf16[2048,2048]{1,0:T(8,128)(2,1)} %w_hbm.1), custom_call_target="tpu_custom_call" | custom-call | tf_op jit(solution)/shard_map/finish/pallas_call | solution.py:317
  57.1 1.9 %copy.7 = bf16[512,512]{1,0:T(8,128)(2,1)} copy(bf16[512,512]{1,0:T(8,128)(2,1)} %finish.1) | data formatting | bytes 1048576

commit v4 on v3

--- a/solution.py
+++ b/solution.py
@@ -94,24 +94,19 @@
 
 
 def pair_rows(ref, p, h):
-    pairs = ref[p * CHUNK : (p + 1) * CHUNK, :, h * WIDTH : (h + 1) * WIDTH]
+    pairs = ref[pl.ds(p * CHUNK, CHUNK), :, h * WIDTH : (h + 1) * WIDTH]
     return pairs.reshape(MICRO, WIDTH)
 
 
-def chunk_kernel(heads, per_step, q_ref, k_ref, v_ref, a_ref, o_ref, map_ref, z_ref):
-    step = pl.program_id(0)
+def advance(step, heads, per_step, k_ref, v_ref, z_ref, start_ref, write_ref):
+    base = step * per_step
     row, col = iota((MICRO, WIDTH), 0), iota((MICRO, WIDTH), 1)
     eye = jnp.where(row == col, 1.0, 0.0).astype(f32)
 
-    @pl.when(step == 0)
-    def _():
-        for h in range(heads):
-            z_ref[h] = jnp.concatenate([eye, jnp.zeros((WIDTH, WIDTH), f32)], axis=1)
-
     where = [(p, h) for p in range(per_step) for h in range(heads)]
 
     def key_of(p, h):
-        return pair_rows(k_ref, p, h)
+        return pair_rows(k_ref, base + p, h)
 
     lowers, scales = [], []
     for p, h in where:
@@ -126,7 +121,7 @@
     prepared = []
     for (p, h), inverse, (down, across) in zip(where, inverses, scales):
         key = key_of(p, h)
-        value = pair_rows(v_ref, p, h)
+        value = pair_rows(v_ref, base + p, h)
         inverse = inverse * (2.0 * down)
         write_key = dot(wide_left(inverse * across), jnp.concatenate([key, key], axis=0))
         write_value = dot(wide_left(inverse), jnp.concatenate([value, value], axis=0))
@@ -136,64 +131,37 @@
         )
         effect = effect[:, : 2 * WIDTH] + effect[:, 2 * WIDTH :]
         move, carry = eye - effect[:, :WIDTH], effect[:, WIDTH:]
-        query = q_ref[p * CHUNK : (p + 1) * CHUNK, h * WIDTH : (h + 1) * WIDTH]
-        scores = dot(query, key, ((1,), (1,)))
-        token, micro = iota((CHUNK, MICRO), 0), iota((CHUNK, MICRO), 1)
-        scores = jnp.where(micro <= 2 * token + 1, scores, 0.0).astype(bf16)
-        inner = dot(scores, jnp.concatenate([wk_high, wv_high], axis=1))
-        query = query.astype(f32)
-        size = lax.rsqrt(jnp.sum(query * query, axis=1, keepdims=True) + epsilon)
-        adjusted = (query - inner[:, :WIDTH]) * size
-        prepared.append((wide_left(move), carry, adjusted.astype(bf16), inner[:, WIDTH:] * size))
-    for (p, h), (move, carry, adjusted, inside) in zip(where, prepared):
-        state = z_ref[h]
-        high, low = split(state)
-        out = dot(adjusted, high)
-        here = (slice(p * CHUNK, (p + 1) * CHUNK), slice(h * WIDTH, (h + 1) * WIDTH))
-        a_ref[here] = out[:, :WIDTH].astype(bf16)
-        o_ref[here] = (out[:, WIDTH:] + inside).astype(o_ref.dtype)
+        write_ref[base + p, h] = jnp.concatenate([wk_high, wv_high], axis=1)
+        prepared.append((wide_left(move), carry))
+    for (p, h), (move, carry) in zip(where, prepared):
+        high, low = split(z_ref[h])
+        start_ref[base + p, h] = high
         both = jnp.concatenate([high, low], axis=1)
         moved = dot(move, jnp.concatenate([both, both], axis=0))
         moved = moved[:, : 2 * WIDTH] + moved[:, 2 * WIDTH :]
         z_ref[h] = jnp.concatenate([moved[:, :WIDTH], moved[:, WIDTH:] + carry], axis=1)
 
-    @pl.when(step == pl.num_programs(0) - 1)
-    def _():
-        map_ref[...] = z_ref[...].astype(map_ref.dtype)
-
-
-def chunk_maps(queries, keys, values, wire):
-    tokens, width = queries.shape
-    heads = width // WIDTH
-    per_step = 2
-    rows = per_step * CHUNK
-    return pl.pallas_call(
-        functools.partial(chunk_kernel, heads, per_step),
-        grid=(tokens // rows,),
-        in_specs=[
-            pl.BlockSpec((rows, width), lambda i: (i, 0)),
-            pl.BlockSpec((rows, 2, width), lambda i: (i, 0, 0)),
-            pl.BlockSpec((rows, 2, width), lambda i: (i, 0, 0)),
-        ],
-        out_specs=[
-            pl.BlockSpec((rows, width), lambda i: (i, 0)),
-            pl.BlockSpec((rows, width), lambda i: (i, 0)),
-            pl.BlockSpec((heads, WIDTH, 2 * WIDTH), lambda i: (0, 0, 0)),
-        ],
-        out_shape=[
-            jax.ShapeDtypeStruct((tokens, width), bf16),
-            jax.ShapeDtypeStruct((tokens, width), f32),
-            jax.ShapeDtypeStruct((heads, WIDTH, 2 * WIDTH), wire),
-        ],
-        scratch_shapes=[pltpu.VMEM((heads, WIDTH, 2 * WIDTH), f32)],
-        compiler_params=pltpu.CompilerParams(vmem_limit_bytes=56 * 2**20),
-        name="chunk_maps",
-    )(queries, keys, values)
-
-
-def finish_kernel(
-    shards, heads, maps_ref, init_ref, a_ref, o_ref, w_hbm, out_ref,
-    w_ref, move_ref, state_ref, wire_out, wire_in, att_ref, acc_ref,
+
+def prepare(chunk, heads, q_ref, k_ref, start_ref, write_ref, a_ref, o_ref):
+    rows = pl.ds(pl.multiple_of(chunk * CHUNK, CHUNK), CHUNK)
+    token, micro = iota((CHUNK, MICRO), 0), iota((CHUNK, MICRO), 1)
+    for h in range(heads):
+        cols = slice(h * WIDTH, (h + 1) * WIDTH)
+        query = q_ref[rows, cols]
+        scores = dot(query, pair_rows(k_ref, chunk, h), ((1,), (1,)))
+        scores = jnp.where(micro <= 2 * token + 1, scores, 0.0).astype(bf16)
+        inner = dot(scores, write_ref[chunk, h])
+        query = query.astype(f32)
+        size = lax.rsqrt(jnp.sum(query * query, axis=1, keepdims=True) + epsilon)
+        adjusted = (query - inner[:, :WIDTH]) * size
+        out = dot(adjusted.astype(bf16), start_ref[chunk, h])
+        a_ref[rows, cols] = out[:, :WIDTH].astype(bf16)
+        o_ref[rows, cols] = out[:, WIDTH:] + inner[:, WIDTH:] * size
+
+
+def layer_kernel(
+    shards, heads, q_ref, k_ref, v_ref, init_ref, w_hbm, out_ref,
+    maps_ref, start_ref, write_ref, a_ref, o_ref, w_ref, move_ref, state_ref, wire_out, wire_in, att_ref, acc_ref,
     w_sem, chain_send, chain_recv, att_send, att_recv,
 ):
     place, group = lax.axis_index("seq"), lax.axis_index("head")
@@ -222,6 +190,20 @@
     def _():
         greet((place + 1, group))
 
+    chunks, per_step = q_ref.shape[0] // CHUNK, 2
+    eye = jnp.where(iota((WIDTH, WIDTH), 0) == iota((WIDTH, WIDTH), 1), 1.0, 0.0).astype(f32)
+    for h in range(heads):
+        maps_ref[h] = jnp.concatenate([eye, jnp.zeros((WIDTH, WIDTH), f32)], axis=1)
+
+    def one_step(step, _):
+        advance(step, heads, per_step, k_ref, v_ref, maps_ref, start_ref, write_ref)
+        return 0
+
+    def one_chunk(chunk, _):
+        prepare(chunk, heads, q_ref, k_ref, start_ref, write_ref, a_ref, o_ref)
+        return 0
+
+    lax.fori_loop(0, chunks // per_step, one_step, 0)
     for h in range(heads):
         move_ref[h] = wide_left(maps_ref[h, :, :WIDTH])
 
@@ -246,31 +228,48 @@
     to_beside = [pass_on(0, 2, h, beside) for h in range(heads)]
     relayed = [pass_on(1, 3, h, beside) for h in range(heads)]
 
-    for h in range(heads):
-
-        @pl.when(place == 0)
-        def _():
-            state_ref[h] = init_ref[h]
-
-        @pl.when(place > 0)
-        def _():
-            chain(h).wait_recv()
-            state_ref[h] = wire_in[h].astype(f32)
-
-        @pl.when(place < shards - 1)
-        def _():
-            both = jnp.concatenate(split(state_ref[h]), axis=1)
-            moved = dot(move_ref[h], jnp.concatenate([both, both], axis=0))
-            moved = moved[:, :WIDTH] + moved[:, WIDTH:] + maps_ref[h, :, WIDTH:]
-            wire_out[h] = moved.astype(wire_out.dtype)
-            chain(h).start()
-
+    def attend(h):
         here = slice(h * WIDTH, (h + 1) * WIDTH)
         att_ref[0, h] = (
             dot(a_ref[:, here], state_ref[h].astype(bf16)) + o_ref[:, here]
         ).astype(bf16)
         to_across[h].start()
         to_beside[h].start()
+
+    late = place >= (shards + 1) // 2
+
+    @pl.when(late)
+    def _():
+        lax.fori_loop(0, chunks, one_chunk, 0)
+
+    for h in range(heads):
+
+        @pl.when(place == 0)
+        def _():
+            state_ref[h] = init_ref[h]
+
+        @pl.when(place > 0)
+        def _():
+            chain(h).wait_recv()
+            state_ref[h] = wire_in[h].astype(f32)
+
+        @pl.when(place < shards - 1)
+        def _():
+            both = jnp.concatenate(split(state_ref[h]), axis=1)
+            moved = dot(move_ref[h], jnp.concatenate([both, both], axis=0))
+            moved = moved[:, :WIDTH] + moved[:, WIDTH:] + maps_ref[h, :, WIDTH:]
+            wire_out[h] = moved.astype(wire_out.dtype)
+            chain(h).start()
+
+        @pl.when(late)
+        def _():
+            attend(h)
+
+    @pl.when(jnp.logical_not(late))
+    def _():
+        lax.fori_loop(0, chunks, one_chunk, 0)
+        for h in range(heads):
+            attend(h)
 
     w_copy.wait()
 
@@ -306,20 +305,26 @@
             chain(h).wait_send()
 
 
-def finish(maps, init_state, a, o, out_weight, wire):
+def layer(queries, key_pairs, value_pairs, init_state, out_weight, wire):
     heads = init_state.shape[0]
     shards = lax.axis_size("seq")
-    tokens = a.shape[0]
+    tokens = queries.shape[0]
+    chunks = tokens // CHUNK
     features = out_weight.shape[0]
     cols = out_weight.shape[1] // lax.axis_size("head")
     vmem = pl.BlockSpec(memory_space=pltpu.VMEM)
     dma = pltpu.SemaphoreType.DMA
     return pl.pallas_call(
-        functools.partial(finish_kernel, shards, heads),
+        functools.partial(layer_kernel, shards, heads),
         in_specs=[vmem] * 4 + [pl.BlockSpec(memory_space=pl.ANY)],
         out_specs=vmem,
         out_shape=jax.ShapeDtypeStruct((tokens, cols), bf16),
         scratch_shapes=[
+            pltpu.VMEM((heads, WIDTH, 2 * WIDTH), f32),
+            pltpu.VMEM((chunks, heads, WIDTH, 2 * WIDTH), bf16),
+            pltpu.VMEM((chunks, heads, MICRO, 2 * WIDTH), bf16),
+            pltpu.VMEM((tokens, heads * WIDTH), bf16),
+            pltpu.VMEM((tokens, heads * WIDTH), f32),
             pltpu.VMEM((features, cols), bf16),
             pltpu.VMEM((heads, WIDTH, 2 * WIDTH), bf16),
             pltpu.VMEM((heads, WIDTH, WIDTH), f32),
@@ -332,14 +337,13 @@
         compiler_params=pltpu.CompilerParams(
             vmem_limit_bytes=56 * 2**20, collective_id=0, has_side_effects=True
         ),
-        name="finish",
-    )(maps, init_state, a, o, out_weight)
+        name="layer",
+    )(queries, key_pairs, value_pairs, init_state, out_weight)
 
 
 def local(queries, key_pairs, value_pairs, init_state, out_weight):
     wire = bf16 if lax.axis_size("seq") <= 8 else f32
-    a, o, maps = chunk_maps(queries, key_pairs, value_pairs, f32)
-    return finish(maps, init_state, a, o, out_weight, wire)
+    return layer(queries, key_pairs, value_pairs, init_state, out_weight, wire)
 
 
 def solution(mesh):

time: 59.2 us -> 50.9 us (0.86)
  Pallas kernels: 57.1 us -> 48.8 us
    pallas_call x2 -> x1, Pallas kernels: 57.1 us -> 48.8 us  [layer(): pl.pallas_call(functools.partial(layer_kernel, shards, heads), in_specs=[...]
where the time goes in v4:
time: 50.9 us; the launch traced here: 50.7 us
  Pallas kernels  48.8 us (96%)
  local copies, waits for them, and re-layouts  1.87 us (4%)
    pallas_call x1, Pallas kernels, layer(): pl.pallas_call(functools.partial(layer_kernel, shards, heads), in_specs=[...  48.8 us
    unnamed x1, local copies, waits for them, and re-layouts  1.87 us

profile of v4, /device:TPU:29, one launch (start us, length us, event | category | flops | bytes accessed | tf_op | source)
XLA Modules:
  0.0 50.7 jit_solution(9938122731654188381)
XLA Ops:
  0.0 48.8 %layer.1 = bf16[512,512]{1,0:T(8,128)(2,1)} custom-call(bf16[512,512]{1,0:T(8,128)(2,1)} %q_ref.1, bf16[512,2,512]{2,1,0:T(2,128)(2,1)} %k_ref.1, bf16[512,2,512]{2,1,0:T(2,128)(2,1)} %v_ref.1, f32[4,128,128]{2,1,0:T(8,128)} %init_ref.1, bf16[2048,2048]{1,0:T(8,128)(2,1)} %w_hbm.1), custom_call_target="tpu_custom_call" | custom-call | tf_op jit(solution)/shard_map/layer/pallas_call | solution.py:317
  48.8 1.9 %copy.7 = bf16[512,512]{1,0:T(8,128)(2,1)} copy(bf16[512,512]{1,0:T(8,128)(2,1)} %layer.1) | data formatting | bytes 1048576

commit v5 on v4

--- a/solution.py
+++ b/solution.py
@@ -190,7 +190,7 @@
     def _():
         greet((place + 1, group))
 
-    chunks, per_step = q_ref.shape[0] // CHUNK, 2
+    chunks, per_step = q_ref.shape[0] // CHUNK, 4
     eye = jnp.where(iota((WIDTH, WIDTH), 0) == iota((WIDTH, WIDTH), 1), 1.0, 0.0).astype(f32)
     for h in range(heads):
         maps_ref[h] = jnp.concatenate([eye, jnp.zeros((WIDTH, WIDTH), f32)], axis=1)

time: 50.9 us -> 49.2 us (0.967)
  Pallas kernels: 48.8 us -> 47.1 us
    pallas_call x1, Pallas kernels: 48.8 us -> 47.1 us  [layer(): pl.pallas_call(functools.partial(layer_kernel, shards, heads), in_specs=[...]
where the time goes in v5:
time: 49.2 us; the launch traced here: 49 us
  Pallas kernels  47.1 us (96%)
  local copies, waits for them, and re-layouts  1.87 us (4%)
    pallas_call x1, Pallas kernels, layer(): pl.pallas_call(functools.partial(layer_kernel, shards, heads), in_specs=[...  47.1 us
    unnamed x1, local copies, waits for them, and re-layouts  1.87 us

profile of v5, /device:TPU:29, one launch (start us, length us, event | category | flops | bytes accessed | tf_op | source)
XLA Modules:
  0.0 49.0 jit_solution(5273695408024072884)
XLA Ops:
  0.0 47.1 %layer.1 = bf16[512,512]{1,0:T(8,128)(2,1)} custom-call(bf16[512,512]{1,0:T(8,128)(2,1)} %q_ref.1, bf16[512,2,512]{2,1,0:T(2,128)(2,1)} %k_ref.1, bf16[512,2,512]{2,1,0:T(2,128)(2,1)} %v_ref.1, f32[4,128,128]{2,1,0:T(8,128)} %init_ref.1, bf16[2048,2048]{1,0:T(8,128)(2,1)} %w_hbm.1), custom_call_target="tpu_custom_call" | custom-call | tf_op jit(solution)/shard_map/layer/pallas_call | solution.py:317
  47.1 1.9 %copy.7 = bf16[512,512]{1,0:T(8,128)(2,1)} copy(bf16[512,512]{1,0:T(8,128)(2,1)} %layer.1) | data formatting | bytes 1048576
